TPU v7x, 32 devices: a whole 2x2x4 slice. The times are simulated.
32 devices in a mesh: ctx: 8 (over z, y), tp: 4 (over x, core).
Axes of the slice: x: 2, y: 2, z: 4, core: 2. Of those that a mesh axis runs over, the one named last changes fastest.
Arguments:
- query: bfloat16 [1024, 8192], P('ctx', 'tp'), may hold values from -6 to 6
- key: bfloat16 [1024, 512], P('ctx', 'tp'), may hold values from -6 to 6
- value: bfloat16 [1024, 512], P('ctx', 'tp'), may hold values from -6 to 6
- out_grad: bfloat16 [1024, 8192], P('ctx', 'tp'), may hold values from -6 to 6
- hidden_in: bfloat16 [1024, 8192], P('ctx', 'tp'), may hold values from -0.119628906 to 0.119628906
- segment_ids: int32 [1024], P('ctx'), may hold values from 0 to 3, as said below
Outputs:
- query_grad: bfloat16 [1024, 8192], P('ctx', 'tp')
- key_grad: bfloat16 [1024, 512], P('ctx', 'tp')
- value_grad: bfloat16 [1024, 512], P('ctx', 'tp')
- value_weight_grad: float32 [8192, 512], P('ctx', 'tp')
Inputs may be any that keep to these rules, and one draw needn't show every extreme that they name: `segment_ids`: ids never fall; document 0 holds 32 to 96 tokens, document 1 exactly 512 tokens, every later document at least one token and fewer than 512.
All inputs are finite; a program needn't handle non-finite values.
Results may differ from a plain program's by a relative error of at most 0.028.
Values may be sent and summed in bfloat16 or wider, within the bound.
A program may use at most 64 MiB of HBM per device.

v0:
```python
import jax
import jax.numpy as jnp
from jax import lax
from jax.sharding import PartitionSpec as P

HD = 128


neg_large = -1e30


def passed_along(block, axis, distance):
    devices = range(lax.axis_size(axis))
    route = [(i - distance, i) for i in devices if i - distance in devices]
    return lax.ppermute(block, axis, route)


def from_behind(value, axis, by):
    length = lax.axis_size(axis)
    return lax.ppermute(value, axis, [(i, (i + by) % length) for i in range(length)])


def on_device(query, key, value, out_grad, hidden_in, segment_ids):
    cycle_size = lax.axis_size("ctx")
    own_index = lax.axis_index("ctx")
    local_rows = query.shape[0]
    kv_heads = key.shape[1] // HD
    group_size = query.shape[1] // HD // kv_heads
    kv_width = key.shape[1]
    score_scale = HD ** (-0.5)
    query_four = query.reshape(local_rows, kv_heads, group_size, HD)
    grad_four = out_grad.reshape(local_rows, kv_heads, group_size, HD)
    offsets = jnp.arange(local_rows, dtype=jnp.int32)
    query_pos = own_index * local_rows + offsets
    first_segment = segment_ids[0]

    def block_mask(block_idx, key_segments):
        key_pos = block_idx * local_rows + offsets
        allowed = (key_pos[None, :] <= query_pos[:, None]) & (
            key_segments[None, :] == segment_ids[:, None]
        )
        is_live = (block_idx <= own_index) & (key_segments[local_rows - 1] >= first_segment)
        return (allowed, is_live)

    def block_scores(pair_block, allowed):
        key_four = pair_block[0].reshape(local_rows, kv_heads, HD)
        scores = (
            jnp.einsum("tkgd,ukd->kgtu", query_four, key_four, preferred_element_type=jnp.float32)
            * score_scale
        )
        return jnp.where(allowed, scores, neg_large)

    def forward_step(running, blocks, block_idx):
        pair_block, key_segments = blocks
        allowed, is_live = block_mask(block_idx, key_segments)

        def forward_work(state):
            peak, total, accum = state
            scores = block_scores(pair_block, allowed)
            new_peak = jnp.maximum(peak, jnp.max(scores, axis=-1))
            weights = jnp.where(allowed, jnp.exp(scores - new_peak[..., None]), 0.0)
            rescale = jnp.exp(peak - new_peak)
            value_four = pair_block[1].reshape(local_rows, kv_heads, HD)
            update = jnp.einsum(
                "kgtu,ukd->kgtd",
                weights.astype(jnp.bfloat16),
                value_four,
                preferred_element_type=jnp.float32,
            )
            return (
                new_peak,
                total * rescale + jnp.sum(weights, axis=-1),
                accum * rescale[..., None] + update,
            )

        return lax.cond(is_live, forward_work, lambda state: state, running)

    def backward_step(blocks, block_idx, log_total, delta):
        pair_block, key_segments = blocks
        allowed, is_live = block_mask(block_idx, key_segments)

        def backward_work(unused):
            scores = block_scores(pair_block, allowed)
            probs = jnp.where(allowed, jnp.exp(scores - log_total[..., None]), 0.0)
            key_four = pair_block[0].reshape(local_rows, kv_heads, HD)
            value_four = pair_block[1].reshape(local_rows, kv_heads, HD)
            dprobs = jnp.einsum(
                "tkgd,ukd->kgtu", grad_four, value_four, preferred_element_type=jnp.float32
            )
            dscores_low = (probs * (dprobs - delta[..., None])).astype(jnp.bfloat16)
            probs_low = probs.astype(jnp.bfloat16)
            query_part = jnp.einsum(
                "kgtu,ukd->tkgd", dscores_low, key_four, preferred_element_type=jnp.float32
            )
            key_part = (
                jnp.einsum(
                    "kgtu,tkgd->ukd", dscores_low, query_four, preferred_element_type=jnp.float32
                )
                * score_scale
            )
            value_part = jnp.einsum(
                "kgtu,tkgd->ukd", probs_low, grad_four, preferred_element_type=jnp.float32
            )
            pair_grads = jnp.stack(
                [key_part.reshape(local_rows, kv_width), value_part.reshape(local_rows, kv_width)]
            )
            return (query_part, pair_grads)

        def skipped(unused):
            return (
                jnp.zeros((local_rows, kv_heads, group_size, HD), jnp.float32),
                jnp.zeros((2, local_rows, kv_width), jnp.float32),
            )

        return lax.cond(is_live, backward_work, skipped, 0)

    pair = jnp.stack([key, value])
    own_blocks = (pair, segment_ids)
    init_running = (
        jnp.full((kv_heads, group_size, local_rows), neg_large, jnp.float32),
        jnp.zeros((kv_heads, group_size, local_rows), jnp.float32),
        jnp.zeros((kv_heads, group_size, local_rows, HD), jnp.float32),
    )
    query_start = jnp.zeros((local_rows, kv_heads, group_size, HD), jnp.float32)

    def cycle_keys(blocks):
        return passed_along((blocks[0], blocks[1]), "ctx", 1)

    def cycle_grads(partial_grads):
        return from_behind(partial_grads.astype(jnp.bfloat16), "ctx", 1).astype(partial_grads.dtype)

    def forward_turn(step_idx, carry):
        blocks, running = carry
        running = forward_step(running, blocks, (own_index - step_idx) % cycle_size)
        return (cycle_keys(blocks), running)

    blocks, running = lax.fori_loop(0, cycle_size - 1, forward_turn, (own_blocks, init_running))
    running = forward_step(running, blocks, (own_index - (cycle_size - 1)) % cycle_size)
    peak, total, accum = running
    finish_log_total = peak + jnp.log(total)
    attn_out = (accum / total[..., None]).astype(jnp.bfloat16)
    finish_delta = jnp.einsum(
        "kgtd,tkgd->kgt", attn_out, grad_four, preferred_element_type=jnp.float32
    )
    log_total = finish_log_total
    delta = finish_delta

    def backward_turn(step_idx, carry):
        blocks, partial_grads, query_acc = carry
        query_part, pair_grads = backward_step(
            blocks, (own_index - step_idx) % cycle_size, log_total, delta
        )
        return (cycle_keys(blocks), cycle_grads(partial_grads + pair_grads), query_acc + query_part)

    grad_start = jnp.zeros((2, local_rows, kv_width), jnp.float32)
    blocks, partial_grads, query_acc = lax.fori_loop(
        0, cycle_size - 1, backward_turn, (own_blocks, grad_start, query_start)
    )
    query_part, pair_grads = backward_step(
        blocks, (own_index - (cycle_size - 1)) % cycle_size, log_total, delta
    )
    finished, query_acc = (partial_grads + pair_grads, query_acc + query_part)
    grads = cycle_grads(finished)
    query_grad = (
        (query_acc * score_scale)
        .astype(jnp.bfloat16)
        .reshape(local_rows, kv_heads * group_size * HD)
    )
    key_grad = grads[0].astype(jnp.bfloat16)
    value_grad = grads[1].astype(jnp.bfloat16)
    columns = lax.all_gather(hidden_in, "tp", axis=1, tiled=True)
    weight_grad = lax.psum_scatter(
        lax.dot_general(
            columns, value_grad, (((0,), (0,)), ((), ())), preferred_element_type=jnp.float32
        ),
        "ctx",
        scatter_dimension=0,
        tiled=True,
    )
    return (query_grad, key_grad, value_grad, weight_grad)


def solution(mesh):
    return jax.shard_map(
        on_device,
        mesh=mesh,
        in_specs=(
            P("ctx", "tp"),
            P("ctx", "tp"),
            P("ctx", "tp"),
            P("ctx", "tp"),
            P("ctx", "tp"),
            P("ctx"),
        ),
        out_specs=(P("ctx", "tp"), P("ctx", "tp"), P("ctx", "tp"), P("ctx", "tp")),
        check_vma=False,
    )
```

profile of v0, /device:TPU:0, one launch (start us, length us, event | category | flops | bytes accessed | tf_op | source)
XLA Modules:
  0.0 351.0 jit_solution(12515164604124904242)
XLA Ops:
  12.0 84.1 %while.46 = (s32[]{:T(128)}, bf16[2,128,128]{2,1,0:T(8,128)(2,1)S(1)}, s32[128]{0:T(128)S(1)}, f32[1,16,128]{2,1,0:T(8,128)S(1)}, f32[1,16,128]{2,1,0:T(8,128)S(...) while((s32[]{:T(128)}, ...), condition=%wide.region_5.6_spmd.clone, body=%wide.region_0.5_spmd.clone.sunk | while | flops 137156880 | bytes 6430748 | solution.py:137
  12.6 4.9 %collective-permute-start = (bf16[2,128,128]{2,1,0:T(8,128)(2,1)}, bf16[2,128,128]{2,1,0:T(8,128)(2,1)S(1)}, u32[]{:S(2)}, u32[]{:S(2)}) collective-permute-start(bf16[2,128,128]{2,1,0:T(8,128)(2,1)} %copy.62), channel_id=1, source_target_pairs={{0,4},{4,8},{8,12},{12,16},{16,20},{20,24},{24,28},{1,5},{5,9},{9,... | collective-permute-start | bytes 196616 | tf_op jit(solution)/shard_map/while/body/eval_jaxpr/ppermute | solution.py:15
  18.0 3.4 collective-permute-start.1
  24.2 3.6 %conditional.10 = ((f32[1,16,128]{2,1,0:T(8,128)S(1)}, f32[1,16,128]{2,1,0:T(8,128)S(1)}, f32[1,16,128,128]{3,2,1,0:T(8,128)S(1)})) conditional(s32[]{:T(128)} %convert_element_type.128, (f32[1,16,128]{2,1,0:T(8,128)S(1)}, f32[1,16,128]{2,1,0:T(8,128)S(1)}, f32[1,16,128,128]{3,2,1,0:T(8,128)S(1)}) %tuple.146, (s32[]{:T(128)}, s32[128]{0:T(128)S(1)}, ...), branch_computations={%region_1.1_spmd, %region_2.4_spmd} | conditional | flops 137156864 | bytes 6033460 | solution.py:76
  28.4 3.4 collective-permute-start
  32.4 3.4 collective-permute-start.1
  39.2 7.0 %collective-permute-start = (bf16[2,128,128]{2,1,0:T(8,128)(2,1)}, bf16[2,128,128]{2,1,0:T(8,128)(2,1)S(1)}, u32[]{:S(2)}, u32[]{:S(2)}) collective-permute-start(bf16[2,128,128]{2,1,0:T(8,128)(2,1)} %copy.62), channel_id=1, source_target_pairs={{0,4},{4,8},{8,12},{12,16},{16,20},{20,24},{24,28},{1,5},{5,9},{9,... | collective-permute-start | bytes 196616 | tf_op jit(solution)/shard_map/while/body/eval_jaxpr/ppermute | solution.py:15
  46.7 3.4 collective-permute-start.1
  53.5 3.4 collective-permute-start
  57.5 5.5 %collective-permute-start.1 = (s32[128]{0:T(128)}, s32[128]{0:T(128)S(1)}, u32[]{:S(2)}, u32[]{:S(2)}) collective-permute-start(s32[128]{0:T(128)} %copy.63), channel_id=1, source_target_pairs={{0,4},{4,8},{8,12},{12,16},{16,20},{20,24},{24,28},{1,5},{5,9},{9,... | collective-permute-start | bytes 1544 | tf_op jit(solution)/shard_map/while/body/eval_jaxpr/ppermute | solution.py:15
  75.9 3.7 %collective-permute-start = (bf16[2,128,128]{2,1,0:T(8,128)(2,1)}, bf16[2,128,128]{2,1,0:T(8,128)(2,1)S(1)}, u32[]{:S(2)}, u32[]{:S(2)}) collective-permute-start(bf16[2,128,128]{2,1,0:T(8,128)(2,1)} %copy.62), channel_id=1, source_target_pairs={{0,4},{4,8},{8,12},{12,16},{16,20},{20,24},{24,28},{1,5},{5,9},{9,... | collective-permute-start | bytes 196616 | tf_op jit(solution)/shard_map/while/body/eval_jaxpr/ppermute | solution.py:15
  80.1 3.7 %collective-permute-start.1 = (s32[128]{0:T(128)}, s32[128]{0:T(128)S(1)}, u32[]{:S(2)}, u32[]{:S(2)}) collective-permute-start(s32[128]{0:T(128)} %copy.63), channel_id=1, source_target_pairs={{0,4},{4,8},{8,12},{12,16},{16,20},{20,24},{24,28},{1,5},{5,9},{9,... | collective-permute-start | bytes 1544 | tf_op jit(solution)/shard_map/while/body/eval_jaxpr/ppermute | solution.py:15
  90.5 2.8 collective-permute-start.1
  107.8 133.0 %while.47 = (s32[]{:T(128)}, bf16[2,128,128]{2,1,0:T(8,128)(2,1)S(1)}, s32[128]{0:T(128)}, f32[2,128,128]{2,1,0:T(8,128)S(1)}, f32[128,1,16,128]{3,0,2,1:T(8,128...) while((s32[]{:T(128)}, ...), condition=%wide.region_13.14_spmd.clone, body=%wide.region_10.13_spmd.clone.sunk | while | flops 338395424 | bytes 12738615 | solution.py:156
  112.4 4.2 %collective-permute-start.3 = (s32[128]{0:T(128)}, s32[128]{0:T(128)}, u32[]{:S(2)}, u32[]{:S(2)}) collective-permute-start(s32[128]{0:T(128)} %copy.88), channel_id=1, source_target_pairs={{0,4},{4,8},{8,12},{12,16},{16,20},{20,24},{24,28},{1,5},{5,9},{9,... | collective-permute-start | bytes 1544 | tf_op jit(solution)/shard_map/while/body/eval_jaxpr/ppermute | solution.py:15
  119.3 4.8 %conditional.11 = (f32[128,1,16,128]{3,0,2,1:T(8,128)S(1)}, f32[2,128,128]{2,1,0:T(8,128)S(1)}) conditional(s32[]{:T(128)} %convert_element_type.130, () %tuple.149, (s32[]{:T(128)}, s32[128]{0:T(128)S(1)}, s32[]{:T(128)}, s32[128]{0:T(128)}, s32[128]{0:T(128)}, /*index=5*/bf16[2,128,128]{2,1,0:T(8,128)(2,1)}, ...), branch_computations={%region_11.11_spmd, %region_12.12_spmd} | conditional | flops 337740032 | bytes 8409124 | solution.py:115
  124.5 6.6 %collective-permute-done.4 = bf16[2,128,128]{2,1,0:T(8,128)(2,1)S(1)} collective-permute-done((bf16[2,128,128]{2,1,0:T(8,128)(2,1)S(1)}, bf16[2,128,128]{2,1,0:T(8,128)(2,1)S(1)}, u32[]{:S(2)}, u32[]{:S(2)}) %collective-permute-start.4) | collective-permute-done | bytes 65568 | tf_op jit(solution)/shard_map/while/body/eval_jaxpr/ppermute | solution.py:20
  138.9 4.0 %collective-permute-start.4 = (bf16[2,128,128]{2,1,0:T(8,128)(2,1)S(1)}, bf16[2,128,128]{2,1,0:T(8,128)(2,1)S(1)}, u32[]{:S(2)}, u32[]{:S(2)}) collective-permute-start(bf16[2,128,128]{2,1,0:T(8,128)(2,1)S(1)} %fusion.99), channel_id=1, source_target_pairs={{0,4},{4,8},{8,12},{12,16},{16,20},{20,24},{24,28},{28,0},{1,5},{5... | collective-permute-start | bytes 196616 | tf_op jit(solution)/shard_map/while/body/eval_jaxpr/ppermute | solution.py:20
  146.6 3.8 %collective-permute-start.2 = (bf16[2,128,128]{2,1,0:T(8,128)(2,1)}, bf16[2,128,128]{2,1,0:T(8,128)(2,1)S(1)}, u32[]{:S(2)}, u32[]{:S(2)}) collective-permute-start(bf16[2,128,128]{2,1,0:T(8,128)(2,1)} %copy.87), channel_id=1, source_target_pairs={{0,4},{4,8},{8,12},{12,16},{16,20},{20,24},{24,28},{1,5},{5,9},{9,... | collective-permute-start | bytes 196616 | tf_op jit(solution)/shard_map/while/body/eval_jaxpr/ppermute | solution.py:15
  157.6 6.6 %collective-permute-done.4 = bf16[2,128,128]{2,1,0:T(8,128)(2,1)S(1)} collective-permute-done((bf16[2,128,128]{2,1,0:T(8,128)(2,1)S(1)}, bf16[2,128,128]{2,1,0:T(8,128)(2,1)S(1)}, u32[]{:S(2)}, u32[]{:S(2)}) %collective-permute-start.4) | collective-permute-done | bytes 65568 | tf_op jit(solution)/shard_map/while/body/eval_jaxpr/ppermute | solution.py:20
  164.9 5.1 %collective-permute-start.2 = (bf16[2,128,128]{2,1,0:T(8,128)(2,1)}, bf16[2,128,128]{2,1,0:T(8,128)(2,1)S(1)}, u32[]{:S(2)}, u32[]{:S(2)}) collective-permute-start(bf16[2,128,128]{2,1,0:T(8,128)(2,1)} %copy.87), channel_id=1, source_target_pairs={{0,4},{4,8},{8,12},{12,16},{16,20},{20,24},{24,28},{1,5},{5,9},{9,... | collective-permute-start | bytes 196616 | tf_op jit(solution)/shard_map/while/body/eval_jaxpr/ppermute | solution.py:15
  171.2 5.7 %collective-permute-start.3 = (s32[128]{0:T(128)}, s32[128]{0:T(128)}, u32[]{:S(2)}, u32[]{:S(2)}) collective-permute-start(s32[128]{0:T(128)} %copy.88), channel_id=1, source_target_pairs={{0,4},{4,8},{8,12},{12,16},{16,20},{20,24},{24,28},{1,5},{5,9},{9,... | collective-permute-start | bytes 1544 | tf_op jit(solution)/shard_map/while/body/eval_jaxpr/ppermute | solution.py:15
  181.1 5.6 %collective-permute-done.4 = bf16[2,128,128]{2,1,0:T(8,128)(2,1)S(1)} collective-permute-done((bf16[2,128,128]{2,1,0:T(8,128)(2,1)S(1)}, bf16[2,128,128]{2,1,0:T(8,128)(2,1)S(1)}, u32[]{:S(2)}, u32[]{:S(2)}) %collective-permute-start.4) | collective-permute-done | bytes 65568 | tf_op jit(solution)/shard_map/while/body/eval_jaxpr/ppermute | solution.py:20
  189.9 5.2 %collective-permute-start.3 = (s32[128]{0:T(128)}, s32[128]{0:T(128)}, u32[]{:S(2)}, u32[]{:S(2)}) collective-permute-start(s32[128]{0:T(128)} %copy.88), channel_id=1, source_target_pairs={{0,4},{4,8},{8,12},{12,16},{16,20},{20,24},{24,28},{1,5},{5,9},{9,... | collective-permute-start | bytes 1544 | tf_op jit(solution)/shard_map/while/body/eval_jaxpr/ppermute | solution.py:15
  200.1 4.8 %collective-permute-done.4 = bf16[2,128,128]{2,1,0:T(8,128)(2,1)S(1)} collective-permute-done((bf16[2,128,128]{2,1,0:T(8,128)(2,1)S(1)}, bf16[2,128,128]{2,1,0:T(8,128)(2,1)S(1)}, u32[]{:S(2)}, u32[]{:S(2)}) %collective-permute-start.4) | collective-permute-done | bytes 65568 | tf_op jit(solution)/shard_map/while/body/eval_jaxpr/ppermute | solution.py:20
  208.1 4.4 %collective-permute-start.3 = (s32[128]{0:T(128)}, s32[128]{0:T(128)}, u32[]{:S(2)}, u32[]{:S(2)}) collective-permute-start(s32[128]{0:T(128)} %copy.88), channel_id=1, source_target_pairs={{0,4},{4,8},{8,12},{12,16},{16,20},{20,24},{24,28},{1,5},{5,9},{9,... | collective-permute-start | bytes 1544 | tf_op jit(solution)/shard_map/while/body/eval_jaxpr/ppermute | solution.py:15
  216.6 5.7 %collective-permute-done.4 = bf16[2,128,128]{2,1,0:T(8,128)(2,1)S(1)} collective-permute-done((bf16[2,128,128]{2,1,0:T(8,128)(2,1)S(1)}, bf16[2,128,128]{2,1,0:T(8,128)(2,1)S(1)}, u32[]{:S(2)}, u32[]{:S(2)}) %collective-permute-start.4) | collective-permute-done | bytes 65568 | tf_op jit(solution)/shard_map/while/body/eval_jaxpr/ppermute | solution.py:20
  225.5 5.4 %collective-permute-start.3 = (s32[128]{0:T(128)}, s32[128]{0:T(128)}, u32[]{:S(2)}, u32[]{:S(2)}) collective-permute-start(s32[128]{0:T(128)} %copy.88), channel_id=1, source_target_pairs={{0,4},{4,8},{8,12},{12,16},{16,20},{20,24},{24,28},{1,5},{5,9},{9,... | collective-permute-start | bytes 1544 | tf_op jit(solution)/shard_map/while/body/eval_jaxpr/ppermute | solution.py:15
  234.1 6.6 %collective-permute-done.4 = bf16[2,128,128]{2,1,0:T(8,128)(2,1)S(1)} collective-permute-done((bf16[2,128,128]{2,1,0:T(8,128)(2,1)S(1)}, bf16[2,128,128]{2,1,0:T(8,128)(2,1)S(1)}, u32[]{:S(2)}, u32[]{:S(2)}) %collective-permute-start.4) | collective-permute-done | bytes 65568 | tf_op jit(solution)/shard_map/while/body/eval_jaxpr/ppermute | solution.py:20
  244.3 7.0 %collective-permute-done.5 = bf16[2,128,128]{2,1,0:T(8,128)(2,1)S(1)} collective-permute-done((bf16[2,128,128]{2,1,0:T(8,128)(2,1)S(1)}, bf16[2,128,128]{2,1,0:T(8,128)(2,1)S(1)}, u32[]{:S(2)}, u32[]{:S(2)}) %collective-permute-start.5) | collective-permute-done | bytes 65568 | tf_op jit(solution)/shard_map/ppermute | solution.py:20
  251.9 4.3 %convolution_bitcast_fusion.10 = f32[8192,128]{0,1:T(8,128)} fusion(bf16[128,128]{1,0:T(8,128)(2,1)S(1)} %get-tuple-element.1058, bf16[128,8192]{1,0:T(8,128)(2,1)} %all-gather.2.cloned.1.call-done), kind=kOutput, calls=%fused_computation.117 | convolution fusion | flops 268435456 | bytes 6324224 | tf_op jit(solution)/shard_map/dot_general | solution.py:173
  258.9 83.3 %reduce-scatter.2.cloned.1.call-done = f32[1024,128]{0,1:T(8,128)} async-done(((f32[8192,128]{0,1:T(8,128)}), f32[1024,128]{0,1:T(8,128)}) %reduce-scatter.2.cloned.1.call-update) | async-done | bytes 524304 | tf_op jit(solution)/shard_map/reduce_scatter | solution.py:172
  (216 shorter events, 102.6 us)
Async XLA Ops:
  7.2 244.7 %all-gather.2.cloned.1.call-start = ((), (), s32[]{:S(2)}) async-start(), calls=%async_computation.1 | async-start | bytes 2621440 | tf_op jit(solution)/shard_map/all_gather | solution.py:171
  7.9 334.2 %reduce-scatter.2.cloned.1.call-start = ((), (), s32[]{:S(2)}) async-start(), calls=%async_computation.2 | async-start | bytes 4718592 | tf_op jit(solution)/shard_map/reduce_scatter | solution.py:172
  12.6 15.1 %collective-permute-start = (bf16[2,128,128]{2,1,0:T(8,128)(2,1)}, bf16[2,128,128]{2,1,0:T(8,128)(2,1)S(1)}, u32[]{:S(2)}, u32[]{:S(2)}) collective-permute-start(bf16[2,128,128]{2,1,0:T(8,128)(2,1)} %copy.62), channel_id=1, source_target_pairs={{0,4},{4,8},{8,12},{12,16},{16,20},{20,24},{24,28},{1,5},{5,9},{9,... | collective-permute-start | bytes 196616 | tf_op jit(solution)/shard_map/while/body/eval_jaxpr/ppermute | solution.py:15
  18.0 9.7 %collective-permute-start.1 = (s32[128]{0:T(128)}, s32[128]{0:T(128)S(1)}, u32[]{:S(2)}, u32[]{:S(2)}) collective-permute-start(s32[128]{0:T(128)} %copy.63), channel_id=1, source_target_pairs={{0,4},{4,8},{8,12},{12,16},{16,20},{20,24},{24,28},{1,5},{5,9},{9,... | collective-permute-start | bytes 1544 | tf_op jit(solution)/shard_map/while/body/eval_jaxpr/ppermute | solution.py:15
  28.4 10.1 %collective-permute-start = (bf16[2,128,128]{2,1,0:T(8,128)(2,1)}, bf16[2,128,128]{2,1,0:T(8,128)(2,1)S(1)}, u32[]{:S(2)}, u32[]{:S(2)}) collective-permute-start(bf16[2,128,128]{2,1,0:T(8,128)(2,1)} %copy.62), channel_id=1, source_target_pairs={{0,4},{4,8},{8,12},{12,16},{16,20},{20,24},{24,28},{1,5},{5,9},{9,... | collective-permute-start | bytes 196616 | tf_op jit(solution)/shard_map/while/body/eval_jaxpr/ppermute | solution.py:15
  39.2 13.7 %collective-permute-start = (bf16[2,128,128]{2,1,0:T(8,128)(2,1)}, bf16[2,128,128]{2,1,0:T(8,128)(2,1)S(1)}, u32[]{:S(2)}, u32[]{:S(2)}) collective-permute-start(bf16[2,128,128]{2,1,0:T(8,128)(2,1)} %copy.62), channel_id=1, source_target_pairs={{0,4},{4,8},{8,12},{12,16},{16,20},{20,24},{24,28},{1,5},{5,9},{9,... | collective-permute-start | bytes 196616 | tf_op jit(solution)/shard_map/while/body/eval_jaxpr/ppermute | solution.py:15
  53.5 12.2 %collective-permute-start = (bf16[2,128,128]{2,1,0:T(8,128)(2,1)}, bf16[2,128,128]{2,1,0:T(8,128)(2,1)S(1)}, u32[]{:S(2)}, u32[]{:S(2)}) collective-permute-start(bf16[2,128,128]{2,1,0:T(8,128)(2,1)} %copy.62), channel_id=1, source_target_pairs={{0,4},{4,8},{8,12},{12,16},{16,20},{20,24},{24,28},{1,5},{5,9},{9,... | collective-permute-start | bytes 196616 | tf_op jit(solution)/shard_map/while/body/eval_jaxpr/ppermute | solution.py:15
  57.5 8.2 %collective-permute-start.1 = (s32[128]{0:T(128)}, s32[128]{0:T(128)S(1)}, u32[]{:S(2)}, u32[]{:S(2)}) collective-permute-start(s32[128]{0:T(128)} %copy.63), channel_id=1, source_target_pairs={{0,4},{4,8},{8,12},{12,16},{16,20},{20,24},{24,28},{1,5},{5,9},{9,... | collective-permute-start | bytes 1544 | tf_op jit(solution)/shard_map/while/body/eval_jaxpr/ppermute | solution.py:15
  66.4 8.9 %collective-permute-start = (bf16[2,128,128]{2,1,0:T(8,128)(2,1)}, bf16[2,128,128]{2,1,0:T(8,128)(2,1)S(1)}, u32[]{:S(2)}, u32[]{:S(2)}) collective-permute-start(bf16[2,128,128]{2,1,0:T(8,128)(2,1)} %copy.62), channel_id=1, source_target_pairs={{0,4},{4,8},{8,12},{12,16},{16,20},{20,24},{24,28},{1,5},{5,9},{9,... | collective-permute-start | bytes 196616 | tf_op jit(solution)/shard_map/while/body/eval_jaxpr/ppermute | solution.py:15
  75.9 10.7 %collective-permute-start = (bf16[2,128,128]{2,1,0:T(8,128)(2,1)}, bf16[2,128,128]{2,1,0:T(8,128)(2,1)S(1)}, u32[]{:S(2)}, u32[]{:S(2)}) collective-permute-start(bf16[2,128,128]{2,1,0:T(8,128)(2,1)} %copy.62), channel_id=1, source_target_pairs={{0,4},{4,8},{8,12},{12,16},{16,20},{20,24},{24,28},{1,5},{5,9},{9,... | collective-permute-start | bytes 196616 | tf_op jit(solution)/shard_map/while/body/eval_jaxpr/ppermute | solution.py:15
  87.2 8.9 %collective-permute-start = (bf16[2,128,128]{2,1,0:T(8,128)(2,1)}, bf16[2,128,128]{2,1,0:T(8,128)(2,1)S(1)}, u32[]{:S(2)}, u32[]{:S(2)}) collective-permute-start(bf16[2,128,128]{2,1,0:T(8,128)(2,1)} %copy.62), channel_id=1, source_target_pairs={{0,4},{4,8},{8,12},{12,16},{16,20},{20,24},{24,28},{1,5},{5,9},{9,... | collective-permute-start | bytes 196616 | tf_op jit(solution)/shard_map/while/body/eval_jaxpr/ppermute | solution.py:15
  108.4 22.7 %collective-permute-start.2 = (bf16[2,128,128]{2,1,0:T(8,128)(2,1)}, bf16[2,128,128]{2,1,0:T(8,128)(2,1)S(1)}, u32[]{:S(2)}, u32[]{:S(2)}) collective-permute-start(bf16[2,128,128]{2,1,0:T(8,128)(2,1)} %copy.87), channel_id=1, source_target_pairs={{0,4},{4,8},{8,12},{12,16},{16,20},{20,24},{24,28},{1,5},{5,9},{9,... | collective-permute-start | bytes 196616 | tf_op jit(solution)/shard_map/while/body/eval_jaxpr/ppermute | solution.py:15
  112.4 18.7 %collective-permute-start.3 = (s32[128]{0:T(128)}, s32[128]{0:T(128)}, u32[]{:S(2)}, u32[]{:S(2)}) collective-permute-start(s32[128]{0:T(128)} %copy.88), channel_id=1, source_target_pairs={{0,4},{4,8},{8,12},{12,16},{16,20},{20,24},{24,28},{1,5},{5,9},{9,... | collective-permute-start | bytes 1544 | tf_op jit(solution)/shard_map/while/body/eval_jaxpr/ppermute | solution.py:15
  124.1 7.0 %collective-permute-start.4 = (bf16[2,128,128]{2,1,0:T(8,128)(2,1)S(1)}, bf16[2,128,128]{2,1,0:T(8,128)(2,1)S(1)}, u32[]{:S(2)}, u32[]{:S(2)}) collective-permute-start(bf16[2,128,128]{2,1,0:T(8,128)(2,1)S(1)} %fusion.99), channel_id=1, source_target_pairs={{0,4},{4,8},{8,12},{12,16},{16,20},{20,24},{24,28},{28,0},{1,5},{5... | collective-permute-start | bytes 196616 | tf_op jit(solution)/shard_map/while/body/eval_jaxpr/ppermute | solution.py:20
  131.8 14.2 %collective-permute-start.2 = (bf16[2,128,128]{2,1,0:T(8,128)(2,1)}, bf16[2,128,128]{2,1,0:T(8,128)(2,1)S(1)}, u32[]{:S(2)}, u32[]{:S(2)}) collective-permute-start(bf16[2,128,128]{2,1,0:T(8,128)(2,1)} %copy.87), channel_id=1, source_target_pairs={{0,4},{4,8},{8,12},{12,16},{16,20},{20,24},{24,28},{1,5},{5,9},{9,... | collective-permute-start | bytes 196616 | tf_op jit(solution)/shard_map/while/body/eval_jaxpr/ppermute | solution.py:15
  134.3 11.6 %collective-permute-start.3 = (s32[128]{0:T(128)}, s32[128]{0:T(128)}, u32[]{:S(2)}, u32[]{:S(2)}) collective-permute-start(s32[128]{0:T(128)} %copy.88), channel_id=1, source_target_pairs={{0,4},{4,8},{8,12},{12,16},{16,20},{20,24},{24,28},{1,5},{5,9},{9,... | collective-permute-start | bytes 1544 | tf_op jit(solution)/shard_map/while/body/eval_jaxpr/ppermute | solution.py:15
  138.9 7.0 %collective-permute-start.4 = (bf16[2,128,128]{2,1,0:T(8,128)(2,1)S(1)}, bf16[2,128,128]{2,1,0:T(8,128)(2,1)S(1)}, u32[]{:S(2)}, u32[]{:S(2)}) collective-permute-start(bf16[2,128,128]{2,1,0:T(8,128)(2,1)S(1)} %fusion.99), channel_id=1, source_target_pairs={{0,4},{4,8},{8,12},{12,16},{16,20},{20,24},{24,28},{28,0},{1,5},{5... | collective-permute-start | bytes 196616 | tf_op jit(solution)/shard_map/while/body/eval_jaxpr/ppermute | solution.py:20
  146.6 17.6 %collective-permute-start.2 = (bf16[2,128,128]{2,1,0:T(8,128)(2,1)}, bf16[2,128,128]{2,1,0:T(8,128)(2,1)S(1)}, u32[]{:S(2)}, u32[]{:S(2)}) collective-permute-start(bf16[2,128,128]{2,1,0:T(8,128)(2,1)} %copy.87), channel_id=1, source_target_pairs={{0,4},{4,8},{8,12},{12,16},{16,20},{20,24},{24,28},{1,5},{5,9},{9,... | collective-permute-start | bytes 196616 | tf_op jit(solution)/shard_map/while/body/eval_jaxpr/ppermute | solution.py:15
  151.7 12.6 %collective-permute-start.3 = (s32[128]{0:T(128)}, s32[128]{0:T(128)}, u32[]{:S(2)}, u32[]{:S(2)}) collective-permute-start(s32[128]{0:T(128)} %copy.88), channel_id=1, source_target_pairs={{0,4},{4,8},{8,12},{12,16},{16,20},{20,24},{24,28},{1,5},{5,9},{9,... | collective-permute-start | bytes 1544 | tf_op jit(solution)/shard_map/while/body/eval_jaxpr/ppermute | solution.py:15
  157.2 7.0 %collective-permute-start.4 = (bf16[2,128,128]{2,1,0:T(8,128)(2,1)S(1)}, bf16[2,128,128]{2,1,0:T(8,128)(2,1)S(1)}, u32[]{:S(2)}, u32[]{:S(2)}) collective-permute-start(bf16[2,128,128]{2,1,0:T(8,128)(2,1)S(1)} %fusion.99), channel_id=1, source_target_pairs={{0,4},{4,8},{8,12},{12,16},{16,20},{20,24},{24,28},{28,0},{1,5},{5... | collective-permute-start | bytes 196616 | tf_op jit(solution)/shard_map/while/body/eval_jaxpr/ppermute | solution.py:20
  164.9 21.9 %collective-permute-start.2 = (bf16[2,128,128]{2,1,0:T(8,128)(2,1)}, bf16[2,128,128]{2,1,0:T(8,128)(2,1)S(1)}, u32[]{:S(2)}, u32[]{:S(2)}) collective-permute-start(bf16[2,128,128]{2,1,0:T(8,128)(2,1)} %copy.87), channel_id=1, source_target_pairs={{0,4},{4,8},{8,12},{12,16},{16,20},{20,24},{24,28},{1,5},{5,9},{9,... | collective-permute-start | bytes 196616 | tf_op jit(solution)/shard_map/while/body/eval_jaxpr/ppermute | solution.py:15
  171.2 15.5 %collective-permute-start.3 = (s32[128]{0:T(128)}, s32[128]{0:T(128)}, u32[]{:S(2)}, u32[]{:S(2)}) collective-permute-start(s32[128]{0:T(128)} %copy.88), channel_id=1, source_target_pairs={{0,4},{4,8},{8,12},{12,16},{16,20},{20,24},{24,28},{1,5},{5,9},{9,... | collective-permute-start | bytes 1544 | tf_op jit(solution)/shard_map/while/body/eval_jaxpr/ppermute | solution.py:15
  179.7 7.0 %collective-permute-start.4 = (bf16[2,128,128]{2,1,0:T(8,128)(2,1)S(1)}, bf16[2,128,128]{2,1,0:T(8,128)(2,1)S(1)}, u32[]{:S(2)}, u32[]{:S(2)}) collective-permute-start(bf16[2,128,128]{2,1,0:T(8,128)(2,1)S(1)} %fusion.99), channel_id=1, source_target_pairs={{0,4},{4,8},{8,12},{12,16},{16,20},{20,24},{24,28},{28,0},{1,5},{5... | collective-permute-start | bytes 196616 | tf_op jit(solution)/shard_map/while/body/eval_jaxpr/ppermute | solution.py:20
  187.4 17.6 %collective-permute-start.2 = (bf16[2,128,128]{2,1,0:T(8,128)(2,1)}, bf16[2,128,128]{2,1,0:T(8,128)(2,1)S(1)}, u32[]{:S(2)}, u32[]{:S(2)}) collective-permute-start(bf16[2,128,128]{2,1,0:T(8,128)(2,1)} %copy.87), channel_id=1, source_target_pairs={{0,4},{4,8},{8,12},{12,16},{16,20},{20,24},{24,28},{1,5},{5,9},{9,... | collective-permute-start | bytes 196616 | tf_op jit(solution)/shard_map/while/body/eval_jaxpr/ppermute | solution.py:15
  189.9 15.0 %collective-permute-start.3 = (s32[128]{0:T(128)}, s32[128]{0:T(128)}, u32[]{:S(2)}, u32[]{:S(2)}) collective-permute-start(s32[128]{0:T(128)} %copy.88), channel_id=1, source_target_pairs={{0,4},{4,8},{8,12},{12,16},{16,20},{20,24},{24,28},{1,5},{5,9},{9,... | collective-permute-start | bytes 1544 | tf_op jit(solution)/shard_map/while/body/eval_jaxpr/ppermute | solution.py:15
  197.9 7.0 %collective-permute-start.4 = (bf16[2,128,128]{2,1,0:T(8,128)(2,1)S(1)}, bf16[2,128,128]{2,1,0:T(8,128)(2,1)S(1)}, u32[]{:S(2)}, u32[]{:S(2)}) collective-permute-start(bf16[2,128,128]{2,1,0:T(8,128)(2,1)S(1)} %fusion.99), channel_id=1, source_target_pairs={{0,4},{4,8},{8,12},{12,16},{16,20},{20,24},{24,28},{28,0},{1,5},{5... | collective-permute-start | bytes 196616 | tf_op jit(solution)/shard_map/while/body/eval_jaxpr/ppermute | solution.py:20
  205.6 16.7 %collective-permute-start.2 = (bf16[2,128,128]{2,1,0:T(8,128)(2,1)}, bf16[2,128,128]{2,1,0:T(8,128)(2,1)S(1)}, u32[]{:S(2)}, u32[]{:S(2)}) collective-permute-start(bf16[2,128,128]{2,1,0:T(8,128)(2,1)} %copy.87), channel_id=1, source_target_pairs={{0,4},{4,8},{8,12},{12,16},{16,20},{20,24},{24,28},{1,5},{5,9},{9,... | collective-permute-start | bytes 196616 | tf_op jit(solution)/shard_map/while/body/eval_jaxpr/ppermute | solution.py:15
  208.1 14.2 %collective-permute-start.3 = (s32[128]{0:T(128)}, s32[128]{0:T(128)}, u32[]{:S(2)}, u32[]{:S(2)}) collective-permute-start(s32[128]{0:T(128)} %copy.88), channel_id=1, source_target_pairs={{0,4},{4,8},{8,12},{12,16},{16,20},{20,24},{24,28},{1,5},{5,9},{9,... | collective-permute-start | bytes 1544 | tf_op jit(solution)/shard_map/while/body/eval_jaxpr/ppermute | solution.py:15
  215.3 7.0 %collective-permute-start.4 = (bf16[2,128,128]{2,1,0:T(8,128)(2,1)S(1)}, bf16[2,128,128]{2,1,0:T(8,128)(2,1)S(1)}, u32[]{:S(2)}, u32[]{:S(2)}) collective-permute-start(bf16[2,128,128]{2,1,0:T(8,128)(2,1)S(1)} %fusion.99), channel_id=1, source_target_pairs={{0,4},{4,8},{8,12},{12,16},{16,20},{20,24},{24,28},{28,0},{1,5},{5... | collective-permute-start | bytes 196616 | tf_op jit(solution)/shard_map/while/body/eval_jaxpr/ppermute | solution.py:20
  223.0 17.8 %collective-permute-start.2 = (bf16[2,128,128]{2,1,0:T(8,128)(2,1)}, bf16[2,128,128]{2,1,0:T(8,128)(2,1)S(1)}, u32[]{:S(2)}, u32[]{:S(2)}) collective-permute-start(bf16[2,128,128]{2,1,0:T(8,128)(2,1)} %copy.87), channel_id=1, source_target_pairs={{0,4},{4,8},{8,12},{12,16},{16,20},{20,24},{24,28},{1,5},{5,9},{9,... | collective-permute-start | bytes 196616 | tf_op jit(solution)/shard_map/while/body/eval_jaxpr/ppermute | solution.py:15
  225.5 15.2 %collective-permute-start.3 = (s32[128]{0:T(128)}, s32[128]{0:T(128)}, u32[]{:S(2)}, u32[]{:S(2)}) collective-permute-start(s32[128]{0:T(128)} %copy.88), channel_id=1, source_target_pairs={{0,4},{4,8},{8,12},{12,16},{16,20},{20,24},{24,28},{1,5},{5,9},{9,... | collective-permute-start | bytes 1544 | tf_op jit(solution)/shard_map/while/body/eval_jaxpr/ppermute | solution.py:15
  233.7 7.0 %collective-permute-start.4 = (bf16[2,128,128]{2,1,0:T(8,128)(2,1)S(1)}, bf16[2,128,128]{2,1,0:T(8,128)(2,1)S(1)}, u32[]{:S(2)}, u32[]{:S(2)}) collective-permute-start(bf16[2,128,128]{2,1,0:T(8,128)(2,1)S(1)} %fusion.99), channel_id=1, source_target_pairs={{0,4},{4,8},{8,12},{12,16},{16,20},{20,24},{24,28},{28,0},{1,5},{5... | collective-permute-start | bytes 196616 | tf_op jit(solution)/shard_map/while/body/eval_jaxpr/ppermute | solution.py:20
  (13 other events, 54.0 us)
Sparse Core Ops, SparseCore 0:
  9.6 25.2 all-gather.1
  256.4 85.7 reduce-scatter.1
where the time goes:
time: 355 us; the launch traced here: 351 us
  waiting for transfers between devices  130 us (37%)
  starting transfers between devices  108 us (30%)
  local copies, waits for them, and re-layouts  59.7 us (17%)
  loops' own time  19.8 us (6%)
  between operations  16.8 us (5%)
  matrix products  10.7 us (3%)
  other arithmetic  7.02 us (2%)
    ppermute x28, starting transfers between devices, passed_along(): return lax.ppermute(block, axis, route)  99.3 us
    reduce_scatter x1, waiting for transfers between devices, on_device(): lax.psum_scatter(lax.dot_general(columns, value_grad, (((0,), (0,)), ((),...  83.3 us
    ppermute x8, waiting for transfers between devices, from_behind(): lax.ppermute(value, axis, [(i, (i + by) % length) for i in range(length)])  45.5 us
    while x28, local copies, waits for them, and re-layouts  21.2 us
    slice x16, local copies, waits for them, and re-layouts, block_mask(): key_segments[local_rows - 1] >= first_segment  20.3 us
    unnamed x24, local copies, waits for them, and re-layouts  15 us
    another operation x1, loops' own time, on_device(): lax.fori_loop(0, cycle_size - 1, forward_turn, (own_blocks, init_running))  9.98 us
    another operation x1, loops' own time, on_device(): lax.fori_loop(0, cycle_size - 1, backward_turn, (own_blocks, grad_start,...  9.36 us
  transfers between devices with their start and end apart: 38, of which 9 were waited for; matrix products, arithmetic and copies ran while one was open for 19% of the time, Pallas kernels for 0%

commit v1 on v0

v1 whole, which is shorter than its diff:
```python
import functools
import math

import jax
import jax.numpy as jnp
from jax import lax
from jax.experimental import pallas as pl
from jax.experimental.pallas import tpu as pltpu
from jax.sharding import PartitionSpec as P

HD = 128
TP = 4
MASKED = -1e30
MESH = pl.DeviceIdType.MESH
SEG_ROWS = 16

NT = (((1,), (1,)), ((), ()))
NN = (((1,), (0,)), ((), ()))


def dot(a, b, dims):
    return lax.dot_general(a, b, dims, preferred_element_type=jnp.float32)


def kernel(
    n, rows, heads, chunks,
    q_hbm, k_hbm, v_hbm, g_hbm, hid_hbm, seg_ref,
    dq_hbm, dk_hbm, dv_hbm, w_hbm,
    q_all, g_all, kv, bias, p_buf, dp_buf, ds_buf, pl_buf, peak, peaks, total, dtotal,
    acc, own, gout, gin, k_t, dq_v, dk_v, vg_all, vg_t, hid, w_v,
    load_sem, kvs, kvr, gs, gr, h1s, h1r, h2s, h2r, vs, vr, out_sem,
):
    half = n // 2
    per_tp = n // TP
    part = rows // TP
    width = w_v.shape[0]
    cw = heads * rows // chunks
    tile = min(256, cw)
    scale = HD ** (-0.5)
    c = lax.axis_index("ctx")
    g = lax.axis_index("tp")
    first = jnp.where(c <= half, 0, half)
    last = jnp.where(c < half, half, n - 1)
    blocks = c - first + 1
    viewers = last - c
    sibling = g + 1 - 2 * (g % 2)
    across = (g + 2) % TP
    sib_across = (sibling + 2) % TP

    k_load = pltpu.make_async_copy(k_hbm, kv.at[0, pl.ds(0, rows)], load_sem.at[0])
    v_load = pltpu.make_async_copy(v_hbm, kv.at[0, pl.ds(rows, rows)], load_sem.at[1])
    k_load.start()
    v_load.start()

    def start_head(h, _):
        cols = pl.ds(pl.multiple_of(h * HD, HD), HD)
        dst = pl.ds(pl.multiple_of(h * rows, rows), rows)
        pltpu.make_async_copy(q_hbm.at[:, cols], q_all.at[dst], load_sem.at[2]).start()
        pltpu.make_async_copy(g_hbm.at[:, cols], g_all.at[dst], load_sem.at[3]).start()
        return 0

    lax.fori_loop(0, heads, start_head, 0)
    seg = seg_ref[...].astype(jnp.float32)
    kv[0, 2 * rows :, :] = jnp.broadcast_to(seg, (SEG_ROWS, rows)).astype(jnp.bfloat16)
    k_load.wait()
    v_load.wait()

    def kv_copy(k, to):
        return pltpu.make_async_remote_copy(
            src_ref=kv.at[0], dst_ref=kv.at[k], send_sem=kvs.at[k], recv_sem=kvr.at[k],
            device_id=(to, g), device_id_type=MESH,
        )

    def kv_send(k, _):
        kv_copy(k, c + k).start()
        return 0

    lax.fori_loop(1, viewers + 1, kv_send, 0)

    def spread_remote(i, q, to):
        return pltpu.make_async_remote_copy(
            src_ref=hid_hbm.at[pl.ds(q * part, part), pl.ds(pl.multiple_of(i * width, width), width)],
            dst_ref=hid.at[c, q], send_sem=h1s.at[i * TP + q], recv_sem=h1r.at[c],
            device_id=(to, q), device_id_type=MESH,
        )

    def spread_local(i, q):
        return pltpu.make_async_copy(
            hid_hbm.at[pl.ds(q * part, part), pl.ds(pl.multiple_of(i * width, width), width)],
            hid.at[c, q], h1r.at[c],
        )

    def spread(s, _):
        i, q = s // TP, s % TP
        to = g * per_tp + i
        mine = (to == c) & (q == g)

        @pl.when(mine)
        def _():
            spread_local(i, q).start()

        @pl.when(jnp.logical_not(mine))
        def _():
            spread_remote(i, q, to).start()

        return 0

    lax.fori_loop(0, n // TP * TP, spread, 0)

    def spread_sent(s, _):
        i, q = s // TP, s % TP
        to = g * per_tp + i

        @pl.when(jnp.logical_not((to == c) & (q == g)))
        def _():
            spread_remote(i, q, to).wait_send()

        return 0

    def spread_arrived(src, _):
        mine = (src == c) & (c // per_tp == g)
        from_tp = c // per_tp

        @pl.when(mine)
        def _():
            pltpu.make_async_copy(
                hid_hbm.at[pl.ds(0, part), pl.ds(0, width)], hid.at[src, g], h1r.at[src]
            ).wait()

        @pl.when(jnp.logical_not(mine))
        def _():
            pltpu.make_async_remote_copy(
                src_ref=hid_hbm.at[pl.ds(0, part), pl.ds(0, width)], dst_ref=hid.at[src, g],
                send_sem=h1s.at[0], recv_sem=h1r.at[src],
                device_id=(src, from_tp), device_id_type=MESH,
            ).wait_recv()

        return 0

    def quarter(which, slot, to):
        return pltpu.make_async_remote_copy(
            src_ref=hid.at[:, which], dst_ref=hid.at[:, which],
            send_sem=h2s.at[slot], recv_sem=h2r.at[slot],
            device_id=(c, to), device_id_type=MESH,
        )

    pltpu.make_async_copy(q_all, q_all, load_sem.at[2]).wait()
    pltpu.make_async_copy(g_all, g_all, load_sem.at[3]).wait()
    row_iota = lax.broadcasted_iota(jnp.int32, (rows, rows), 0)
    col_iota = lax.broadcasted_iota(jnp.int32, (rows, rows), 1)

    if chunks > 1:
        acc[...] = jnp.zeros_like(acc)

        def all_arrived(k, _):
            kv_copy(k, c).wait_recv()
            return 0

        lax.fori_loop(1, blocks, all_arrived, 0)

    def clear(k, _):
        ds_buf[pl.ds(pl.multiple_of(k * rows, rows), rows), :] = jnp.zeros((rows, cw), jnp.bfloat16)
        k_t[k] = jnp.zeros((HD, rows), jnp.bfloat16)
        return 0

    lax.fori_loop(blocks, half + 1, clear, 0)

    def grad_copy(k, to):
        return pltpu.make_async_remote_copy(
            src_ref=gout.at[k], dst_ref=gin.at[k], send_sem=gs.at[k], recv_sem=gr.at[k],
            device_id=(to, g), device_id_type=MESH,
        )

    def one_chunk(chunk):
        base = 0 if chunks == 1 else pl.multiple_of(chunk * cw, cw)
        peak[...] = jnp.full_like(peak, MASKED)
        total[...] = jnp.zeros_like(total)
        dtotal[...] = jnp.zeros_like(dtotal)

        def forward(k, _):
            if chunks == 1:
                @pl.when(k > 0)
                def _():
                    kv_copy(k, c).wait_recv()

            key_seg = kv[k, 2 * rows : 2 * rows + SEG_ROWS, :][0:1, :].astype(jnp.float32)
            seg_u = jnp.broadcast_to(key_seg, (rows, rows)).T
            allowed = (seg_u == seg) & (row_iota <= col_iota + k * rows)
            one_bias = jnp.where(allowed, 0.0, MASKED)
            bias[...] = jnp.concatenate([one_bias] * (tile // rows), axis=1)
            k_t[k] = kv[k, :rows, :].T
            for at in range(0, cw, tile):
                cols = slice(at, at + tile)
                from_rows = pl.ds(base + at, tile)
                s = dot(kv[k, :rows, :], q_all[from_rows, :], NT) * (scale * math.log2(math.e)) + bias[...]
                dp = dot(kv[k, rows : 2 * rows, :], g_all[from_rows, :], NT)
                old = peak[:, cols]
                new = jnp.maximum(old, jnp.max(s, axis=0, keepdims=True))
                p = jnp.exp2(s - new)
                shrink = jnp.exp2(old - new)
                total[:, cols] = total[:, cols] * shrink + jnp.sum(p, axis=0, keepdims=True)
                dtotal[:, cols] = dtotal[:, cols] * shrink + jnp.sum(p * dp, axis=0, keepdims=True)
                peak[:, cols] = new
                peaks[k, :, cols] = new
                p_buf[k, :, cols] = p
                dp_buf[k, :, cols] = dp
            return 0

        lax.fori_loop(0, blocks, forward, 0)

        if chunks == 1:
            lax.fori_loop(0, n, spread_arrived, 0)
            quarter(g, 0, across).start()
            quarter(g, 1, sibling).start()

        total[...] = 1.0 / total[...]
        dtotal[...] = dtotal[...] * total[...]

        def backward(step, _):
            k = blocks - 1 - step
            ds_rows = pl.ds(pl.multiple_of(k * rows, rows), rows)
            for at in range(0, cw, tile):
                cols = slice(at, at + tile)
                factor = jnp.exp2(peaks[k, :, cols] - peak[:, cols]) * total[:, cols]
                p = p_buf[k, :, cols] * factor
                ds = p * (dp_buf[k, :, cols] - dtotal[:, cols])
                pl_buf[:, cols] = p.astype(jnp.bfloat16)
                ds_buf[ds_rows, cols] = ds.astype(jnp.bfloat16)
            dk = dot(ds_buf[ds_rows, :], q_all[pl.ds(base, cw), :], NN) * scale
            dv = dot(pl_buf[...], g_all[pl.ds(base, cw), :], NN)
            if chunks > 1:
                acc[k, :rows, :] += dk
                acc[k, rows:, :] += dv
            else:
                @pl.when(k > 0)
                def _():
                    gout[k, :rows, :] = dk.astype(jnp.bfloat16)
                    gout[k, rows:, :] = dv.astype(jnp.bfloat16)
                    grad_copy(k, c - k).start()

                @pl.when(k == 0)
                def _():
                    own[:rows, :] = dk
                    own[rows:, :] = dv
            return 0

        lax.fori_loop(0, blocks, backward, 0)

    def query_part(chunk):
        base = 0 if chunks == 1 else pl.multiple_of(chunk * cw, cw)
        k_flat = jnp.concatenate([k_t[k] for k in range(half + 1)], axis=1)
        for at in range(0, cw, tile):
            part_t = dot(k_flat, ds_buf[:, at : at + tile], NN) * scale
            for j in range(0, tile, rows):
                cols = pl.ds(pl.multiple_of(base + at + j, HD), HD)
                dq_v[:, cols] = part_t[:, j : j + rows].T.astype(jnp.bfloat16)

    if chunks == 1:
        one_chunk(0)
        query_part(0)
    else:
        def chunk_step(chunk, _):
            one_chunk(chunk)
            query_part(chunk)
            return 0

        lax.fori_loop(0, chunks, chunk_step, 0)

        def send_grads(step, _):
            k = blocks - 1 - step
            gout[k] = acc[k].astype(jnp.bfloat16)
            grad_copy(k, c - k).start()
            return 0

        lax.fori_loop(0, blocks - 1, send_grads, 0)
        own[...] = acc[0]
        lax.fori_loop(0, n, spread_arrived, 0)
        quarter(g, 0, across).start()
        quarter(g, 1, sibling).start()

    dq_out = pltpu.make_async_copy(dq_v, dq_hbm, out_sem.at[0])
    dq_out.start()

    def add_grads(k, _):
        grad_copy(k, c).wait_recv()
        own[...] += gin[k].astype(jnp.float32)
        return 0

    lax.fori_loop(1, viewers + 1, add_grads, 0)
    vg_all[c] = own[rows:, :].astype(jnp.bfloat16)

    def vg_copy(to, slot):
        return pltpu.make_async_remote_copy(
            src_ref=vg_all.at[slot], dst_ref=vg_all.at[slot], send_sem=vs.at[to], recv_sem=vr.at[slot],
            device_id=(to, g), device_id_type=MESH,
        )

    def vg_send(o, _):
        vg_copy((c + o) % n, c).start()
        return 0

    lax.fori_loop(1, n, vg_send, 0)
    dk_v[...] = own[:rows, :].astype(jnp.bfloat16)
    dk_out = pltpu.make_async_copy(dk_v, dk_hbm, out_sem.at[1])
    dk_out.start()
    dv_out = pltpu.make_async_copy(vg_all.at[c], dv_hbm, out_sem.at[2])
    dv_out.start()

    quarter(across, 0, across).wait_recv()
    quarter(across, 2, sibling).start()
    vg_t[c] = vg_all[c].T

    def vg_arrived(o, _):
        src = (c + o) % n
        vg_copy(src, src).wait_recv()
        vg_t[src] = vg_all[src].T
        return 0

    lax.fori_loop(1, n, vg_arrived, 0)
    quarter(sibling, 1, sibling).wait_recv()
    quarter(sib_across, 2, sibling).wait_recv()

    wt = min(256, width)
    vg_flat = jnp.concatenate([vg_t[j] for j in range(n)], axis=1)
    for at in range(0, width, wt):
        columns = hid[:, :, :, at : at + wt].reshape(n * rows, wt)
        w_t = dot(vg_flat, columns, NN)
        w_v[at : at + wt, :] = w_t.T
    w_out = pltpu.make_async_copy(w_v, w_hbm, out_sem.at[3])
    w_out.start()

    def kv_sent(k, _):
        kv_copy(k, c + k).wait_send()
        return 0

    def grads_sent(k, _):
        grad_copy(k, c - k).wait_send()
        return 0

    def vg_sent(o, _):
        vg_copy((c + o) % n, c).wait_send()
        return 0

    lax.fori_loop(1, viewers + 1, kv_sent, 0)
    lax.fori_loop(0, n // TP * TP, spread_sent, 0)
    lax.fori_loop(1, blocks, grads_sent, 0)
    lax.fori_loop(1, n, vg_sent, 0)
    quarter(g, 0, across).wait_send()
    quarter(g, 1, sibling).wait_send()
    quarter(across, 2, sibling).wait_send()
    dq_out.wait()
    dk_out.wait()
    dv_out.wait()
    w_out.wait()


def on_device(n, query, key, value, out_grad, hidden_in, segment_ids):
    rows = query.shape[0]
    heads = query.shape[1] // HD
    half = n // 2
    width = hidden_in.shape[1] * TP // n
    chunks = 1
    while (half + 1) * rows * (heads * rows // chunks) * 8 > 12 * 2**20 and heads * rows // chunks > 256:
        chunks *= 2
    cw = heads * rows // chunks
    bf, f32 = jnp.bfloat16, jnp.float32
    dma = pltpu.SemaphoreType.DMA
    vmem = pltpu.VMEM
    any_spec = pl.BlockSpec(memory_space=pl.ANY)
    acc_blocks = half + 1 if chunks > 1 else 1
    return pl.pallas_call(
        functools.partial(kernel, n, rows, heads, chunks),
        out_shape=(
            jax.ShapeDtypeStruct(query.shape, bf),
            jax.ShapeDtypeStruct(key.shape, bf),
            jax.ShapeDtypeStruct(value.shape, bf),
            jax.ShapeDtypeStruct((width, HD), f32),
        ),
        in_specs=[any_spec] * 5 + [pl.BlockSpec(memory_space=pltpu.VMEM)],
        out_specs=(any_spec,) * 4,
        scratch_shapes=[
            vmem((heads * rows, HD), bf),
            vmem((heads * rows, HD), bf),
            vmem((half + 1, 2 * rows + SEG_ROWS, HD), bf),
            vmem((rows, min(256, cw)), f32),
            vmem((half + 1, rows, cw), f32),
            vmem((half + 1, rows, cw), f32),
            vmem(((half + 1) * rows, cw), bf),
            vmem((rows, cw), bf),
            vmem((1, cw), f32),
            vmem((half + 1, 1, cw), f32),
            vmem((1, cw), f32),
            vmem((1, cw), f32),
            vmem((acc_blocks, 2 * rows, HD), f32),
            vmem((2 * rows, HD), f32),
            vmem((half + 1, 2 * rows, HD), bf),
            vmem((half + 1, 2 * rows, HD), bf),
            vmem((half + 1, HD, rows), bf),
            vmem((rows, heads * HD), bf),
            vmem((rows, HD), bf),
            vmem((n, rows, HD), bf),
            vmem((n, HD, rows), bf),
            vmem((n, TP, rows // TP, width), bf),
            vmem((width, HD), f32),
            dma((4,)),
            dma((half + 1,)),
            dma((half + 1,)),
            dma((half + 1,)),
            dma((half + 1,)),
            dma((n,)),
            dma((n,)),
            dma((3,)),
            dma((3,)),
            dma((n,)),
            dma((n,)),
            dma((4,)),
        ],
        compiler_params=pltpu.CompilerParams(
            has_side_effects=True, vmem_limit_bytes=48 * 2**20
        ),
        cost_estimate=pl.CostEstimate(flops=4 * 10**9, bytes_accessed=4 * 2**20, transcendentals=2**21),
    )(query, key, value, out_grad, hidden_in, segment_ids.reshape(1, rows))


def solution(mesh):
    return jax.shard_map(
        functools.partial(on_device, mesh.shape["ctx"]),
        mesh=mesh,
        in_specs=(
            P("ctx", "tp"),
            P("ctx", "tp"),
            P("ctx", "tp"),
            P("ctx", "tp"),
            P("ctx", "tp"),
            P("ctx"),
        ),
        out_specs=(P("ctx", "tp"), P("ctx", "tp"), P("ctx", "tp"), P("ctx", "tp")),
        check_vma=False,
    )
```

time: 355 us -> 58.9 us (0.17)
  the two profiles are of different devices: /device:TPU:0 before, /device:TPU:21 now
where the time goes in v1:
time: 58.9 us; the launch traced here: 58.5 us
  Pallas kernels  49.8 us (85%)
  local copies, waits for them, and re-layouts  8.1 us (14%)
  between operations  0.66 us (1%)
    pallas_call x1, Pallas kernels, on_device(): pl.pallas_call(functools.partial(kernel, n, rows, heads, chunks), out_sha...  49.8 us
    unnamed x16, local copies, waits for them, and re-layouts  8.1 us

profile of v1, /device:TPU:21, one launch (start us, length us, event | category | flops | bytes accessed | tf_op | source)
XLA Modules:
  0.0 58.5 jit_solution(10339381895794216383)
XLA Ops:
  0.6 0.0 copy-start.5
  0.6 0.6 %copy-done.5 = s32[128]{0:T(128)S(1)} copy-done((s32[128]{0:T(128)S(1)}, s32[128]{0:T(128)}, u32[]{:S(2)}) %copy-start.5) | copy-done | bytes 536
  1.3 0.0 copy-start
  1.3 1.0 %copy-done = bf16[128,2048]{1,0:T(8,128)(2,1)S(1)} copy-done((bf16[128,2048]{1,0:T(8,128)(2,1)S(1)}, bf16[128,2048]{1,0:T(8,128)(2,1)}, u32[]{:S(2)}) %copy-start) | copy-done | bytes 524312
  2.3 0.0 copy-start.1
  2.3 1.0 %copy-done.1 = bf16[128,2048]{1,0:T(8,128)(2,1)S(1)} copy-done((bf16[128,2048]{1,0:T(8,128)(2,1)S(1)}, bf16[128,2048]{1,0:T(8,128)(2,1)}, u32[]{:S(2)}) %copy-start.1) | copy-done | bytes 524312
  3.4 0.0 copy-start.2
  3.4 1.0 %copy-done.2 = bf16[128,2048]{1,0:T(8,128)(2,1)S(1)} copy-done((bf16[128,2048]{1,0:T(8,128)(2,1)S(1)}, bf16[128,2048]{1,0:T(8,128)(2,1)}, u32[]{:S(2)}) %copy-start.2) | copy-done | bytes 524312
  4.4 0.0 copy-start.3
  4.4 0.8 %copy-done.3 = bf16[128,128]{1,0:T(8,128)(2,1)S(1)} copy-done((bf16[128,128]{1,0:T(8,128)(2,1)S(1)}, bf16[128,128]{1,0:T(8,128)(2,1)}, u32[]{:S(2)}) %copy-start.3) | copy-done | bytes 32792
  5.2 0.0 copy-start.4
  5.2 0.8 %copy-done.4 = bf16[128,128]{1,0:T(8,128)(2,1)S(1)} copy-done((bf16[128,128]{1,0:T(8,128)(2,1)S(1)}, bf16[128,128]{1,0:T(8,128)(2,1)}, u32[]{:S(2)}) %copy-start.4) | copy-done | bytes 32792
  5.9 49.8 %shard_map.93 = (bf16[128,2048]{1,0:T(8,128)(2,1)S(1)}, bf16[128,128]{1,0:T(8,128)(2,1)S(1)}, bf16[128,128]{1,0:T(8,128)(2,1)S(1)}, f32[1024,128]{1,0:T(8,128)S(1)}) custom-call(bf16[128,2048]{1,0:T(8,128)(2,1)S(1)} %copy-done, bf16[128,128]{1,0:T(8,128)(2,1)S(1)} %copy-done.3, bf16[128,128]{1,0:T(8,128)(2,1)S(1)} %copy-done.4, ...), custom_call_target="tpu_custom_call" | custom-call | flops 4000000000 | bytes 4194304 | tf_op jit(solution)/shard_map/pallas_call | solution.py:371
  55.7 0.8 %copy.14 = bf16[128,2048]{1,0:T(8,128)(2,1)} copy(bf16[128,2048]{1,0:T(8,128)(2,1)S(1)} %get-tuple-element.8) | data formatting | bytes 1048576
  56.5 0.6 %copy.15 = bf16[128,128]{1,0:T(8,128)(2,1)} copy(bf16[128,128]{1,0:T(8,128)(2,1)S(1)} %get-tuple-element.9) | data formatting | bytes 65536
  57.1 0.6 %copy.16 = bf16[128,128]{1,0:T(8,128)(2,1)} copy(bf16[128,128]{1,0:T(8,128)(2,1)S(1)} %get-tuple-element.10) | data formatting | bytes 65536
  57.7 0.8 %copy.17 = f32[1024,128]{1,0:T(8,128)} copy(f32[1024,128]{1,0:T(8,128)S(1)} %get-tuple-element.11) | data formatting | bytes 1048576
Async XLA Ops:
  0.6 0.7 %copy-start.5 = (s32[128]{0:T(128)S(1)}, s32[128]{0:T(128)}, u32[]{:S(2)}) copy-start(s32[128]{0:T(128)} %param.11) | copy-start | bytes 1540
  1.3 1.0 %copy-start = (bf16[128,2048]{1,0:T(8,128)(2,1)S(1)}, bf16[128,2048]{1,0:T(8,128)(2,1)}, u32[]{:S(2)}) copy-start(bf16[128,2048]{1,0:T(8,128)(2,1)} %q_hbm.1) | copy-start | bytes 1572868
  2.3 1.0 %copy-start.1 = (bf16[128,2048]{1,0:T(8,128)(2,1)S(1)}, bf16[128,2048]{1,0:T(8,128)(2,1)}, u32[]{:S(2)}) copy-start(bf16[128,2048]{1,0:T(8,128)(2,1)} %g_hbm.1) | copy-start | bytes 1572868
  3.4 1.0 %copy-start.2 = (bf16[128,2048]{1,0:T(8,128)(2,1)S(1)}, bf16[128,2048]{1,0:T(8,128)(2,1)}, u32[]{:S(2)}) copy-start(bf16[128,2048]{1,0:T(8,128)(2,1)} %hid_hbm.1) | copy-start | bytes 1572868
  4.4 0.8 %copy-start.3 = (bf16[128,128]{1,0:T(8,128)(2,1)S(1)}, bf16[128,128]{1,0:T(8,128)(2,1)}, u32[]{:S(2)}) copy-start(bf16[128,128]{1,0:T(8,128)(2,1)} %k_hbm.1) | copy-start | bytes 98308
  5.2 0.8 %copy-start.4 = (bf16[128,128]{1,0:T(8,128)(2,1)S(1)}, bf16[128,128]{1,0:T(8,128)(2,1)}, u32[]{:S(2)}) copy-start(bf16[128,128]{1,0:T(8,128)(2,1)} %v_hbm.1) | copy-start | bytes 98308

commit v2 on v1

--- a/solution.py
+++ b/solution.py
@@ -47,6 +47,17 @@
     across = (g + 2) % TP
     sib_across = (sibling + 2) % TP
 
+    barrier = pltpu.get_barrier_semaphore()
+
+    def greet(d, _):
+        @pl.when(d != c * TP + g)
+        def _():
+            pl.semaphore_signal(barrier, inc=1, device_id=(d // TP, d % TP), device_id_type=MESH)
+
+        return 0
+
+    lax.fori_loop(0, n * TP, greet, 0)
+
     k_load = pltpu.make_async_copy(k_hbm, kv.at[0, pl.ds(0, rows)], load_sem.at[0])
     v_load = pltpu.make_async_copy(v_hbm, kv.at[0, pl.ds(rows, rows)], load_sem.at[1])
     k_load.start()
@@ -64,6 +75,7 @@
     kv[0, 2 * rows :, :] = jnp.broadcast_to(seg, (SEG_ROWS, rows)).astype(jnp.bfloat16)
     k_load.wait()
     v_load.wait()
+    pl.semaphore_wait(barrier, n * TP - 1)
 
     def kv_copy(k, to):
         return pltpu.make_async_remote_copy(
@@ -90,7 +102,8 @@
             hid.at[c, q], h1r.at[c],
         )
 
-    def spread(s, _):
+    def spread(step, _):
+        s = (step + c * (TP + 1)) % (n // TP * TP)
         i, q = s // TP, s % TP
         to = g * per_tp + i
         mine = (to == c) & (q == g)
@@ -208,11 +221,6 @@
 
         lax.fori_loop(0, blocks, forward, 0)
 
-        if chunks == 1:
-            lax.fori_loop(0, n, spread_arrived, 0)
-            quarter(g, 0, across).start()
-            quarter(g, 1, sibling).start()
-
         total[...] = 1.0 / total[...]
         dtotal[...] = dtotal[...] * total[...]
 
@@ -274,12 +282,13 @@
 
         lax.fori_loop(0, blocks - 1, send_grads, 0)
         own[...] = acc[0]
-        lax.fori_loop(0, n, spread_arrived, 0)
-        quarter(g, 0, across).start()
-        quarter(g, 1, sibling).start()
 
     dq_out = pltpu.make_async_copy(dq_v, dq_hbm, out_sem.at[0])
     dq_out.start()
+
+    lax.fori_loop(0, n, spread_arrived, 0)
+    quarter(g, 0, across).start()
+    quarter(g, 1, sibling).start()
 
     def add_grads(k, _):
         grad_copy(k, c).wait_recv()
@@ -368,7 +377,7 @@
     vmem = pltpu.VMEM
     any_spec = pl.BlockSpec(memory_space=pl.ANY)
     acc_blocks = half + 1 if chunks > 1 else 1
-    return pl.pallas_call(
+    results = pl.pallas_call(
         functools.partial(kernel, n, rows, heads, chunks),
         out_shape=(
             jax.ShapeDtypeStruct(query.shape, bf),
@@ -416,10 +425,11 @@
             dma((4,)),
         ],
         compiler_params=pltpu.CompilerParams(
-            has_side_effects=True, vmem_limit_bytes=48 * 2**20
+            has_side_effects=True, vmem_limit_bytes=62 * 2**20, collective_id=0
         ),
         cost_estimate=pl.CostEstimate(flops=4 * 10**9, bytes_accessed=4 * 2**20, transcendentals=2**21),
     )(query, key, value, out_grad, hidden_in, segment_ids.reshape(1, rows))
+    return results
 
 
 def solution(mesh):

time: 58.9 us -> 53.1 us (0.902)
  the two profiles are of different devices: /device:TPU:21 before, /device:TPU:0 now
where the time goes in v2:
time: 53.1 us; the launch traced here: 52.8 us
  Pallas kernels  48.1 us (91%)
  local copies, waits for them, and re-layouts  4.13 us (8%)
  between operations  0.66 us (1%)
    pallas_call x1, Pallas kernels, on_device(): pl.pallas_call(functools.partial(kernel, n, rows, heads, chunks), out_sha...  48.1 us
    unnamed x10, local copies, waits for them, and re-layouts  4.13 us

profile of v2, /device:TPU:0, one launch (start us, length us, event | category | flops | bytes accessed | tf_op | source)
XLA Modules:
  0.0 52.8 jit_solution(7258835997875138043)
XLA Ops:
  0.6 48.1 %shard_map.93 = (bf16[128,2048]{1,0:T(8,128)(2,1)}, bf16[128,128]{1,0:T(8,128)(2,1)}, bf16[128,128]{1,0:T(8,128)(2,1)}, f32[1024,128]{1,0:T(8,128)}) custom-call(bf16[128,2048]{1,0:T(8,128)(2,1)} %q_hbm.1, bf16[128,128]{1,0:T(8,128)(2,1)} %k_hbm.1, bf16[128,128]{1,0:T(8,128)(2,1)} %v_hbm.1, bf16[128,2048]{1,0:T(8,128)(2,1)} %g_hbm.1, ...), custom_call_target="tpu_custom_call" | custom-call | flops 4000000000 | bytes 4194304 | tf_op jit(solution)/shard_map/pallas_call | solution.py:380
  48.7 0.0 copy-start.2
  48.7 0.0 copy-start
  48.7 1.9 %copy.14 = bf16[128,2048]{1,0:T(8,128)(2,1)} copy(bf16[128,2048]{1,0:T(8,128)(2,1)} %get-tuple-element.8) | data formatting | bytes 1048576
  50.7 0.0 copy-done.2
  50.7 0.0 copy-start.1
  50.7 0.6 %copy.15 = bf16[128,128]{1,0:T(8,128)(2,1)} copy(bf16[128,128]{1,0:T(8,128)(2,1)S(1)} %copy-done.2) | data formatting | bytes 65536
  51.3 0.2 copy-done.1
  51.4 0.6 %copy.16 = bf16[128,128]{1,0:T(8,128)(2,1)} copy(bf16[128,128]{1,0:T(8,128)(2,1)S(1)} %copy-done.1) | data formatting | bytes 65536
  52.0 0.0 copy-done
  52.0 0.8 %copy.17 = f32[1024,128]{1,0:T(8,128)} copy(f32[1024,128]{1,0:T(8,128)S(1)} %copy-done) | data formatting | bytes 1048576
Async XLA Ops:
  48.7 2.0 %copy-start.2 = (bf16[128,128]{1,0:T(8,128)(2,1)S(1)}, bf16[128,128]{1,0:T(8,128)(2,1)}, u32[]{:S(2)}) copy-start(bf16[128,128]{1,0:T(8,128)(2,1)} %get-tuple-element.9) | copy-start | bytes 98308
  48.7 3.3 %copy-start = (f32[1024,128]{1,0:T(8,128)S(1)}, f32[1024,128]{1,0:T(8,128)}, u32[]{:S(2)}) copy-start(f32[1024,128]{1,0:T(8,128)} %get-tuple-element.11) | copy-start | bytes 1572868
  50.7 0.8 %copy-start.1 = (bf16[128,128]{1,0:T(8,128)(2,1)S(1)}, bf16[128,128]{1,0:T(8,128)(2,1)}, u32[]{:S(2)}) copy-start(bf16[128,128]{1,0:T(8,128)(2,1)} %get-tuple-element.10) | copy-start | bytes 98308

commit v3 on v2

--- a/solution.py
+++ b/solution.py
@@ -150,10 +150,13 @@
 
         return 0
 
-    def quarter(which, slot, to):
+    near = c // half * half
+
+    def quarter(which, slot, to, turn):
+        sources = pl.ds(near if turn == 0 else half - near, half)
         return pltpu.make_async_remote_copy(
-            src_ref=hid.at[:, which], dst_ref=hid.at[:, which],
-            send_sem=h2s.at[slot], recv_sem=h2r.at[slot],
+            src_ref=hid.at[sources, which], dst_ref=hid.at[sources, which],
+            send_sem=h2s.at[3 * turn + slot], recv_sem=h2r.at[3 * turn + slot],
             device_id=(c, to), device_id_type=MESH,
         )
 
@@ -265,6 +268,9 @@
 
     if chunks == 1:
         one_chunk(0)
+        lax.fori_loop(near, near + half, spread_arrived, 0)
+        quarter(g, 0, across, 0).start()
+        quarter(g, 1, sibling, 0).start()
         query_part(0)
     else:
         def chunk_step(chunk, _):
@@ -282,13 +288,16 @@
 
         lax.fori_loop(0, blocks - 1, send_grads, 0)
         own[...] = acc[0]
+        lax.fori_loop(near, near + half, spread_arrived, 0)
+        quarter(g, 0, across, 0).start()
+        quarter(g, 1, sibling, 0).start()
 
     dq_out = pltpu.make_async_copy(dq_v, dq_hbm, out_sem.at[0])
     dq_out.start()
 
-    lax.fori_loop(0, n, spread_arrived, 0)
-    quarter(g, 0, across).start()
-    quarter(g, 1, sibling).start()
+    lax.fori_loop(half - near, n - near, spread_arrived, 0)
+    quarter(g, 0, across, 1).start()
+    quarter(g, 1, sibling, 1).start()
 
     def add_grads(k, _):
         grad_copy(k, c).wait_recv()
@@ -315,8 +324,10 @@
     dv_out = pltpu.make_async_copy(vg_all.at[c], dv_hbm, out_sem.at[2])
     dv_out.start()
 
-    quarter(across, 0, across).wait_recv()
-    quarter(across, 2, sibling).start()
+    quarter(across, 0, across, 0).wait_recv()
+    quarter(across, 2, sibling, 0).start()
+    quarter(across, 0, across, 1).wait_recv()
+    quarter(across, 2, sibling, 1).start()
     vg_t[c] = vg_all[c].T
 
     def vg_arrived(o, _):
@@ -326,8 +337,10 @@
         return 0
 
     lax.fori_loop(1, n, vg_arrived, 0)
-    quarter(sibling, 1, sibling).wait_recv()
-    quarter(sib_across, 2, sibling).wait_recv()
+    quarter(sibling, 1, sibling, 0).wait_recv()
+    quarter(sibling, 1, sibling, 1).wait_recv()
+    quarter(sib_across, 2, sibling, 0).wait_recv()
+    quarter(sib_across, 2, sibling, 1).wait_recv()
 
     wt = min(256, width)
     vg_flat = jnp.concatenate([vg_t[j] for j in range(n)], axis=1)
@@ -354,9 +367,12 @@
     lax.fori_loop(0, n // TP * TP, spread_sent, 0)
     lax.fori_loop(1, blocks, grads_sent, 0)
     lax.fori_loop(1, n, vg_sent, 0)
-    quarter(g, 0, across).wait_send()
-    quarter(g, 1, sibling).wait_send()
-    quarter(across, 2, sibling).wait_send()
+    quarter(g, 0, across, 0).wait_send()
+    quarter(g, 0, across, 1).wait_send()
+    quarter(g, 1, sibling, 0).wait_send()
+    quarter(g, 1, sibling, 1).wait_send()
+    quarter(across, 2, sibling, 0).wait_send()
+    quarter(across, 2, sibling, 1).wait_send()
     dq_out.wait()
     dk_out.wait()
     dv_out.wait()
@@ -418,8 +434,8 @@
             dma((half + 1,)),
             dma((n,)),
             dma((n,)),
-            dma((3,)),
-            dma((3,)),
+            dma((6,)),
+            dma((6,)),
             dma((n,)),
             dma((n,)),
             dma((4,)),

time: 53.1 us -> 51.3 us (0.966)
  Pallas kernels: 48.1 us -> 46.3 us
    pallas_call x1, Pallas kernels: 48.1 us -> 46.3 us  [on_device(): pl.pallas_call(functools.partial(kernel, n, rows, heads, chunks), out_sha...]
where the time goes in v3:
time: 51.3 us; the launch traced here: 51 us
  Pallas kernels  46.3 us (90%)
  local copies, waits for them, and re-layouts  4.13 us (8%)
  between operations  0.66 us (1%)
    pallas_call x1, Pallas kernels, on_device(): pl.pallas_call(functools.partial(kernel, n, rows, heads, chunks), out_sha...  46.3 us
    unnamed x10, local copies, waits for them, and re-layouts  4.13 us

profile of v3, /device:TPU:0, one launch (start us, length us, event | category | flops | bytes accessed | tf_op | source)
XLA Modules:
  0.0 51.0 jit_solution(17756582116307295512)
XLA Ops:
  0.6 46.3 %shard_map.93 = (bf16[128,2048]{1,0:T(8,128)(2,1)}, bf16[128,128]{1,0:T(8,128)(2,1)}, bf16[128,128]{1,0:T(8,128)(2,1)}, f32[1024,128]{1,0:T(8,128)}) custom-call(bf16[128,2048]{1,0:T(8,128)(2,1)} %q_hbm.1, bf16[128,128]{1,0:T(8,128)(2,1)} %k_hbm.1, bf16[128,128]{1,0:T(8,128)(2,1)} %v_hbm.1, bf16[128,2048]{1,0:T(8,128)(2,1)} %g_hbm.1, ...), custom_call_target="tpu_custom_call" | custom-call | flops 4000000000 | bytes 4194304 | tf_op jit(solution)/shard_map/pallas_call | solution.py:396
  46.9 0.0 copy-start.2
  46.9 0.0 copy-start
  46.9 1.9 %copy.14 = bf16[128,2048]{1,0:T(8,128)(2,1)} copy(bf16[128,2048]{1,0:T(8,128)(2,1)} %get-tuple-element.8) | data formatting | bytes 1048576
  48.9 0.0 copy-done.2
  48.9 0.0 copy-start.1
  48.9 0.6 %copy.15 = bf16[128,128]{1,0:T(8,128)(2,1)} copy(bf16[128,128]{1,0:T(8,128)(2,1)S(1)} %copy-done.2) | data formatting | bytes 65536
  49.5 0.2 copy-done.1
  49.6 0.6 %copy.16 = bf16[128,128]{1,0:T(8,128)(2,1)} copy(bf16[128,128]{1,0:T(8,128)(2,1)S(1)} %copy-done.1) | data formatting | bytes 65536
  50.2 0.0 copy-done
  50.2 0.8 %copy.17 = f32[1024,128]{1,0:T(8,128)} copy(f32[1024,128]{1,0:T(8,128)S(1)} %copy-done) | data formatting | bytes 1048576
Async XLA Ops:
  46.9 2.0 %copy-start.2 = (bf16[128,128]{1,0:T(8,128)(2,1)S(1)}, bf16[128,128]{1,0:T(8,128)(2,1)}, u32[]{:S(2)}) copy-start(bf16[128,128]{1,0:T(8,128)(2,1)} %get-tuple-element.9) | copy-start | bytes 98308
  46.9 3.3 %copy-start = (f32[1024,128]{1,0:T(8,128)S(1)}, f32[1024,128]{1,0:T(8,128)}, u32[]{:S(2)}) copy-start(f32[1024,128]{1,0:T(8,128)} %get-tuple-element.11) | copy-start | bytes 1572868
  48.9 0.8 %copy-start.1 = (bf16[128,128]{1,0:T(8,128)(2,1)S(1)}, bf16[128,128]{1,0:T(8,128)(2,1)}, u32[]{:S(2)}) copy-start(bf16[128,128]{1,0:T(8,128)(2,1)} %get-tuple-element.10) | copy-start | bytes 98308
